TPU v7x, 256 devices: a whole 4x4x8 slice. The times are simulated.
256 devices in a mesh: leaf: 32 (over y, z), sub: 8 (over x, core).
Axes of the slice: x: 4, y: 4, z: 8, core: 2. Of those that a mesh axis runs over, the one named last changes fastest.
Arguments:
- rhs: float32 [8, 32, 1024, 128], P('sub', 'leaf'), may hold values from -6 to 6
- leaf_block: bfloat16 [8, 32, 1024, 1024], P('sub', 'leaf')
- leaf_inverse: bfloat16 [8, 32, 1024, 1024], P('sub', 'leaf')
- level_basis: float32 [8, 32, 5, 1024, 128], P('sub', 'leaf'), may hold values from -0.1875 to 0.1875
- level_core: float32 [8, 32, 5, 128, 128], P('sub', 'leaf')
- skeleton_basis: float32 [8, 32, 1024, 128], P('sub', 'leaf'), may hold values from -0.1875 to 0.1875
- coupling: float32 [8, 8, 128, 128], P('sub'), may hold values from -0.09375 to 0.09375
Outputs:
- solution: float32 [8, 32, 1024, 128], P('sub', 'leaf')
All inputs are finite; a program needn't handle non-finite values.
Results may differ from a plain program's by a relative error of at most 0.0003.
Values sent between devices are 32-bit elements; how exact they have to be, the bound alone decides.
A program may use at most 64 MiB of HBM per device.

v0:
```python
import jax
import jax.numpy as jnp
from jax import lax
from jax.sharding import PartitionSpec as P

ROUNDS = 2
HI = lax.Precision.HIGHEST


def partner(x, axis, stride):
    return lax.ppermute(x, axis, [(i, i ^ 1 << stride) for i in range(lax.axis_size(axis))])


def matmul(left, right):
    return jnp.dot(left, right, precision=HI, preferred_element_type=jnp.float32)


def tmatmul(left, right):
    return lax.dot_general(
        left, right, (((0,), (0,)), ((), ())), precision=HI, preferred_element_type=jnp.float32
    )


def group_sum(proj, level):
    total = proj
    for bit_num in range(level + 1):
        total = total + partner(total, "leaf", bit_num)
    return total


def inner_solve(field, inverse, basis, core):
    x = matmul(inverse, field)
    depth = lax.axis_size("leaf").bit_length() - 1
    for level in range(depth):
        proj = tmatmul(basis[level], x)
        group = group_sum(proj, level)
        x = x - matmul(basis[level], matmul(core[level], group))
    return x


def body(rhs, leaf_block, leaf_inverse, level_basis, level_core, skeleton_basis, coupling):
    target = rhs[0, 0]
    block = leaf_block[0, 0].astype(jnp.float32)
    inverse = leaf_inverse[0, 0].astype(jnp.float32)
    basis = level_basis[0, 0]
    core = level_core[0, 0]
    skeleton = skeleton_basis[0, 0]
    row_coupling = coupling[0]
    solution = inner_solve(target, inverse, basis, core)
    for outer in range(ROUNDS):
        local_skel = tmatmul(skeleton, solution)
        subtree_total = lax.psum(local_skel, "leaf")
        every_skel = lax.all_gather(subtree_total[None], "sub", axis=0, tiled=True)
        mixed = jnp.einsum(
            "tkj,tjr->kr",
            row_coupling,
            every_skel,
            precision=HI,
            preferred_element_type=jnp.float32,
        )
        applied = matmul(block, solution) + matmul(skeleton, mixed)
        solution = solution + inner_solve(target - applied, inverse, basis, core)
    return solution[None, None]


def solution(mesh):
    return jax.shard_map(
        body,
        mesh=mesh,
        in_specs=(
            P("sub", "leaf", None, None),
            P("sub", "leaf", None, None),
            P("sub", "leaf", None, None),
            P("sub", "leaf", None, None, None),
            P("sub", "leaf", None, None, None),
            P("sub", "leaf", None, None),
            P("sub", None, None, None),
        ),
        out_specs=P("sub", "leaf", None, None),
        check_vma=False,
    )
```

profile of v0, /device:TPU:8, one launch (start us, length us, event | category | flops | bytes accessed | tf_op | source)
XLA Modules:
  0.0 641.4 jit_solution(17399125690273079579)
XLA Ops:
  40.6 7.6 %collective-permute-start.5 = (f32[128,128]{0,1:T(8,128)S(1)}, f32[128,128]{0,1:T(8,128)S(1)}, u32[]{:S(2)}, u32[]{:S(2)}) collective-permute-start(f32[128,128]{0,1:T(8,128)S(1)} %add.161), channel_id=1, source_target_pairs={{0,32},{8,40},{16,48},{24,56},{32,0},{40,8},{48,16},{56,24},{64,96... | collective-permute-start | bytes 196616 | tf_op jit(solution)/shard_map/ppermute | solution.py:11
  58.4 5.2 collective-permute-done.7
  63.6 5.3 collective-permute-start.8
  78.2 5.1 collective-permute-done.10
  88.5 4.7 collective-permute-start.12
  109.6 139.8 %all-reduce.3.cloned.1.call-done = f32[1,128,128]{1,2,0:T(8,128)} async-done(((f32[1,128,128]{1,2,0:T(8,128)}), f32[1,128,128]{1,2,0:T(8,128)}) %all-reduce.3.cloned.1.call-update) | async-done | bytes 65552 | tf_op jit(solution)/shard_map/psum | solution.py:52
  250.4 14.0 %all_gather.6 = f32[8,128,128]{2,1,0:T(8,128)S(1)} all-gather(f32[1,128,128]{2,1,0:T(8,128)S(1)} %copy.30), channel_id=1, replica_groups=mesh['leaf'=32,'sub'=8] {'sub'}, dimensions={0}, use_global_device_ids=true | all-gather | bytes 589824 | tf_op jit(solution)/shard_map/all_gather | solution.py:53
  304.5 4.2 collective-permute-start.20
  308.7 4.1 collective-permute-done.20
  329.7 5.1 collective-permute-done.23
  335.0 4.3 collective-permute-done.24
  354.2 6.2 collective-permute-done.27
  365.7 4.9 collective-permute-done.29
  374.0 136.5 %all-reduce.5.cloned.1.call-done = f32[1,128,128]{1,2,0:T(8,128)} async-done(((f32[1,128,128]{1,2,0:T(8,128)}), f32[1,128,128]{1,2,0:T(8,128)}) %all-reduce.5.cloned.1.call-update) | async-done | bytes 65552 | tf_op jit(solution)/shard_map/psum | solution.py:52
  511.5 13.8 %all_gather.7 = f32[8,128,128]{2,1,0:T(8,128)S(1)} all-gather(f32[1,128,128]{2,1,0:T(8,128)S(1)} %copy.37), channel_id=1, replica_groups=mesh['leaf'=32,'sub'=8] {'sub'}, dimensions={0}, use_global_device_ids=true | all-gather | bytes 589824 | tf_op jit(solution)/shard_map/all_gather | solution.py:53
  562.7 5.2 collective-permute-done.34
  569.8 6.8 %collective-permute-done.35 = f32[128,128]{0,1:T(8,128)S(1)} collective-permute-done((f32[128,128]{0,1:T(8,128)S(1)}, f32[128,128]{0,1:T(8,128)S(1)}, u32[]{:S(2)}, u32[]{:S(2)}) %collective-permute-start.35) | collective-permute-done | bytes 65568 | tf_op jit(solution)/shard_map/ppermute | solution.py:11
  578.6 4.3 collective-permute-done.36
  583.7 4.7 collective-permute-done.37
  590.9 6.5 %collective-permute-done.38 = f32[128,128]{0,1:T(8,128)S(1)} collective-permute-done((f32[128,128]{0,1:T(8,128)S(1)}, f32[128,128]{0,1:T(8,128)S(1)}, u32[]{:S(2)}, u32[]{:S(2)}) %collective-permute-start.38) | collective-permute-done | bytes 65568 | tf_op jit(solution)/shard_map/ppermute | solution.py:11
  603.8 4.3 collective-permute-done.40
  608.5 5.4 collective-permute-done.41
  615.7 6.5 %collective-permute-done.42 = f32[128,128]{0,1:T(8,128)S(1)} collective-permute-done((f32[128,128]{0,1:T(8,128)S(1)}, f32[128,128]{0,1:T(8,128)S(1)}, u32[]{:S(2)}, u32[]{:S(2)}) %collective-permute-start.42) | collective-permute-done | bytes 65568 | tf_op jit(solution)/shard_map/ppermute | solution.py:11
  628.0 4.5 collective-permute-done.44
  (188 shorter events, 218.0 us)
Async XLA Ops:
  6.5 242.9 %all-reduce.3.cloned.1.call-start = ((), (), s32[]{:S(2)}) async-start(), calls=%async_computation | async-start | bytes 131072 | tf_op jit(solution)/shard_map/psum | solution.py:52
  22.8 5.6 collective-permute-start.2
  40.6 9.8 %collective-permute-start.5 = (f32[128,128]{0,1:T(8,128)S(1)}, f32[128,128]{0,1:T(8,128)S(1)}, u32[]{:S(2)}, u32[]{:S(2)}) collective-permute-start(f32[128,128]{0,1:T(8,128)S(1)} %add.161), channel_id=1, source_target_pairs={{0,32},{8,40},{16,48},{24,56},{32,0},{40,8},{48,16},{56,24},{64,96... | collective-permute-start | bytes 196616 | tf_op jit(solution)/shard_map/ppermute | solution.py:11
  56.9 6.6 %collective-permute-start.7 = (f32[128,128]{0,1:T(8,128)S(1)}, f32[128,128]{0,1:T(8,128)S(1)}, u32[]{:S(2)}, u32[]{:S(2)}) collective-permute-start(f32[128,128]{0,1:T(8,128)S(1)} %add.163), channel_id=1, source_target_pairs={{0,16},{8,24},{16,0},{24,8},{32,48},{40,56},{48,32},{56,40},{64,80... | collective-permute-start | bytes 196616 | tf_op jit(solution)/shard_map/ppermute | solution.py:11
  63.6 8.3 %collective-permute-start.8 = (f32[128,128]{0,1:T(8,128)S(1)}, f32[128,128]{0,1:T(8,128)S(1)}, u32[]{:S(2)}, u32[]{:S(2)}) collective-permute-start(f32[128,128]{0,1:T(8,128)S(1)} %add.164), channel_id=1, source_target_pairs={{0,32},{8,40},{16,48},{24,56},{32,0},{40,8},{48,16},{56,24},{64,96... | collective-permute-start | bytes 196616 | tf_op jit(solution)/shard_map/ppermute | solution.py:11
  88.5 8.3 %collective-permute-start.12 = (f32[128,128]{0,1:T(8,128)S(1)}, f32[128,128]{0,1:T(8,128)S(1)}, u32[]{:S(2)}, u32[]{:S(2)}) collective-permute-start(f32[128,128]{0,1:T(8,128)S(1)} %add.168), channel_id=1, source_target_pairs={{0,32},{8,40},{16,48},{24,56},{32,0},{40,8},{48,16},{56,24},{64,96... | collective-permute-start | bytes 196616 | tf_op jit(solution)/shard_map/ppermute | solution.py:11
  101.2 5.9 collective-permute-start.14
  109.6 401.0 %all-reduce.5.cloned.1.call-start = ((), (), s32[]{:S(2)}) async-start(), calls=%async_computation.1 | async-start | bytes 131072 | tf_op jit(solution)/shard_map/psum | solution.py:52
  287.6 5.3 collective-permute-start.17
  299.2 5.3 collective-permute-start.19
  304.5 8.3 %collective-permute-start.20 = (f32[128,128]{0,1:T(8,128)S(1)}, f32[128,128]{0,1:T(8,128)S(1)}, u32[]{:S(2)}, u32[]{:S(2)}) collective-permute-start(f32[128,128]{0,1:T(8,128)S(1)} %add.178), channel_id=1, source_target_pairs={{0,32},{8,40},{16,48},{24,56},{32,0},{40,8},{48,16},{56,24},{64,96... | collective-permute-start | bytes 196616 | tf_op jit(solution)/shard_map/ppermute | solution.py:11
  319.4 6.2 collective-permute-start.22
  325.6 9.2 %collective-permute-start.23 = (f32[128,128]{0,1:T(8,128)S(1)}, f32[128,128]{0,1:T(8,128)S(1)}, u32[]{:S(2)}, u32[]{:S(2)}) collective-permute-start(f32[128,128]{0,1:T(8,128)S(1)} %add.181), channel_id=1, source_target_pairs={{0,32},{8,40},{16,48},{24,56},{32,0},{40,8},{48,16},{56,24},{64,96... | collective-permute-start | bytes 196616 | tf_op jit(solution)/shard_map/ppermute | solution.py:11
  345.5 6.0 collective-permute-start.26
  351.5 9.0 %collective-permute-start.27 = (f32[128,128]{0,1:T(8,128)S(1)}, f32[128,128]{0,1:T(8,128)S(1)}, u32[]{:S(2)}, u32[]{:S(2)}) collective-permute-start(f32[128,128]{0,1:T(8,128)S(1)} %add.185), channel_id=1, source_target_pairs={{0,32},{8,40},{16,48},{24,56},{32,0},{40,8},{48,16},{56,24},{64,96... | collective-permute-start | bytes 196616 | tf_op jit(solution)/shard_map/ppermute | solution.py:11
  364.8 5.9 collective-permute-start.29
  555.9 5.3 collective-permute-start.33
  561.2 6.7 %collective-permute-start.34 = (f32[128,128]{0,1:T(8,128)S(1)}, f32[128,128]{0,1:T(8,128)S(1)}, u32[]{:S(2)}, u32[]{:S(2)}) collective-permute-start(f32[128,128]{0,1:T(8,128)S(1)} %add.195), channel_id=1, source_target_pairs={{0,16},{8,24},{16,0},{24,8},{32,48},{40,56},{48,32},{56,40},{64,80... | collective-permute-start | bytes 196616 | tf_op jit(solution)/shard_map/ppermute | solution.py:11
  567.9 8.7 %collective-permute-start.35 = (f32[128,128]{0,1:T(8,128)S(1)}, f32[128,128]{0,1:T(8,128)S(1)}, u32[]{:S(2)}, u32[]{:S(2)}) collective-permute-start(f32[128,128]{0,1:T(8,128)S(1)} %add.196), channel_id=1, source_target_pairs={{0,32},{8,40},{16,48},{24,56},{32,0},{40,8},{48,16},{56,24},{64,96... | collective-permute-start | bytes 196616 | tf_op jit(solution)/shard_map/ppermute | solution.py:11
  582.9 5.6 collective-permute-start.37
  588.5 8.9 %collective-permute-start.38 = (f32[128,128]{0,1:T(8,128)S(1)}, f32[128,128]{0,1:T(8,128)S(1)}, u32[]{:S(2)}, u32[]{:S(2)}) collective-permute-start(f32[128,128]{0,1:T(8,128)S(1)} %add.199), channel_id=1, source_target_pairs={{0,32},{8,40},{16,48},{24,56},{32,0},{40,8},{48,16},{56,24},{64,96... | collective-permute-start | bytes 196616 | tf_op jit(solution)/shard_map/ppermute | solution.py:11
  608.0 6.0 collective-permute-start.41
  614.0 8.3 %collective-permute-start.42 = (f32[128,128]{0,1:T(8,128)S(1)}, f32[128,128]{0,1:T(8,128)S(1)}, u32[]{:S(2)}, u32[]{:S(2)}) collective-permute-start(f32[128,128]{0,1:T(8,128)S(1)} %add.203), channel_id=1, source_target_pairs={{0,32},{8,40},{16,48},{24,56},{32,0},{40,8},{48,16},{56,24},{64,96... | collective-permute-start | bytes 196616 | tf_op jit(solution)/shard_map/ppermute | solution.py:11
  626.6 5.9 collective-permute-start.44
  (35 other events, 389.6 us)
Sparse Core Ops, SparseCore 0:
  109.7 139.6 all-reduce.2
  374.1 136.3 all-reduce.4
where the time goes:
time: 651 us; the launch traced here: 641 us
  waiting for transfers between devices  450 us (69%)
  starting transfers between devices  83.4 us (13%)
  matrix products  57.5 us (9%)
  blocking collectives  27.7 us (4%)
  between operations  14.4 us (2%)
  local copies, waits for them, and re-layouts  8.09 us (1%)
    psum x2, waiting for transfers between devices, body(): subtree_total = lax.psum(local_skel, 'leaf')  276 us
    ppermute x45, waiting for transfers between devices, partner(): lax.ppermute(x, axis, [(i, i ^ 1 << stride) for i in range(lax.axis_size(...  174 us
    ppermute x45, starting transfers between devices, partner(): lax.ppermute(x, axis, [(i, i ^ 1 << stride) for i in range(lax.axis_size(...  83.4 us
    dot_general x37, matrix products, matmul(): jnp.dot(left, right, precision=HI, preferred_element_type=jnp.float32)  31.4 us
    all_gather x2, blocking collectives, body(): every_skel = lax.all_gather(subtree_total[None], 'sub', axis=0, tiled=True)  27.7 us
    dot_general x17, matrix products, tmatmul(): lax.dot_general(left, right, (((0,), (0,)), ((), ())), precision=HI, pref...  22 us
  transfers between devices with their start and end apart: 47, of which 47 were waited for; matrix products, arithmetic and copies ran while one was open for 0% of the time, Pallas kernels for 0%

commit v1 on v0

--- a/solution.py
+++ b/solution.py
@@ -49,7 +49,7 @@
     solution = inner_solve(target, inverse, basis, core)
     for outer in range(ROUNDS):
         local_skel = tmatmul(skeleton, solution)
-        subtree_total = lax.psum(local_skel, "leaf")
+        subtree_total = jnp.sum(lax.all_gather(local_skel, "leaf"), axis=0)
         every_skel = lax.all_gather(subtree_total[None], "sub", axis=0, tiled=True)
         mixed = jnp.einsum(
             "tkj,tjr->kr",

time: 651 us -> 521 us (0.80)
  waiting for transfers between devices: 450 us -> 303 us
  starting transfers between devices: 83.4 us -> 102 us
    psum x2 -> x0, waiting for transfers between devices: 276 us -> none  [body(): subtree_total = lax.psum(local_skel, 'leaf')]
    all_gather x0 -> x2, waiting for transfers between devices: none -> 149 us  [body(): subtree_total = jnp.sum(lax.all_gather(local_skel, 'leaf'), axis=0)]
    ppermute x45, waiting for transfers between devices: 174 us -> 154 us  [partner(): lax.ppermute(x, axis, [(i, i ^ 1 << stride) for i in range(lax.axis_size(...]
    ppermute x45, starting transfers between devices: 83.4 us -> 102 us  [partner(): lax.ppermute(x, axis, [(i, i ^ 1 << stride) for i in range(lax.axis_size(...]
  transfers between devices with their start and end apart: 47 -> 47, of which waited for: 47 -> 47; matrix products, arithmetic and copies ran while one was open for 0% -> 1% of each run, Pallas kernels for 0% -> 0%
where the time goes in v1:
time: 521 us; the launch traced here: 512 us
  waiting for transfers between devices  303 us (58%)
  starting transfers between devices  102 us (20%)
  matrix products  53.5 us (10%)
  blocking collectives  27.7 us (5%)
  between operations  14.4 us (3%)
  local copies, waits for them, and re-layouts  10.3 us (2%)
    ppermute x45, waiting for transfers between devices, partner(): lax.ppermute(x, axis, [(i, i ^ 1 << stride) for i in range(lax.axis_size(...  154 us
    all_gather x2, waiting for transfers between devices, body(): subtree_total = jnp.sum(lax.all_gather(local_skel, 'leaf'), axis=0)  149 us
    ppermute x45, starting transfers between devices, partner(): lax.ppermute(x, axis, [(i, i ^ 1 << stride) for i in range(lax.axis_size(...  102 us
    dot_general x37, matrix products, matmul(): jnp.dot(left, right, precision=HI, preferred_element_type=jnp.float32)  30.3 us
    all_gather x2, blocking collectives, body(): every_skel = lax.all_gather(subtree_total[None], 'sub', axis=0, tiled=True)  27.7 us
    dot_general x17, matrix products, tmatmul(): lax.dot_general(left, right, (((0,), (0,)), ((), ())), precision=HI, pref...  22 us
  transfers between devices with their start and end apart: 47, of which 47 were waited for; matrix products, arithmetic and copies ran while one was open for 1% of the time, Pallas kernels for 0%

profile of v1, /device:TPU:8, one launch (start us, length us, event | category | flops | bytes accessed | tf_op | source)
XLA Modules:
  0.0 511.7 jit_solution(12410502471732345382)
XLA Ops:
  40.6 7.6 %collective-permute-start.5 = (f32[128,128]{0,1:T(8,128)S(1)}, f32[128,128]{0,1:T(8,128)S(1)}, u32[]{:S(2)}, u32[]{:S(2)}) collective-permute-start(f32[128,128]{0,1:T(8,128)S(1)} %add.157), channel_id=1, source_target_pairs={{0,32},{8,40},{16,48},{24,56},{32,0},{40,8},{48,16},{56,24},{64,96... | collective-permute-start | bytes 196616 | tf_op jit(solution)/shard_map/ppermute | solution.py:11
  53.2 3.7 collective-permute-done.6
  58.4 5.2 %collective-permute-done.7 = f32[128,128]{0,1:T(8,128)S(1)} collective-permute-done((f32[128,128]{0,1:T(8,128)S(1)}, f32[128,128]{0,1:T(8,128)S(1)}, u32[]{:S(2)}, u32[]{:S(2)}) %collective-permute-start.7) | collective-permute-done | bytes 65568 | tf_op jit(solution)/shard_map/ppermute | solution.py:11
  63.6 5.3 %collective-permute-start.8 = (f32[128,128]{0,1:T(8,128)S(1)}, f32[128,128]{0,1:T(8,128)S(1)}, u32[]{:S(2)}, u32[]{:S(2)}) collective-permute-start(f32[128,128]{0,1:T(8,128)S(1)} %add.160), channel_id=1, source_target_pairs={{0,32},{8,40},{16,48},{24,56},{32,0},{40,8},{48,16},{56,24},{64,96... | collective-permute-start | bytes 196616 | tf_op jit(solution)/shard_map/ppermute | solution.py:11
  78.2 5.1 collective-permute-done.10
  84.4 4.1 collective-permute-done.11
  88.5 4.7 collective-permute-start.12
  109.6 75.6 %all-gather.7.cloned.1.call-done = f32[4096,128]{0,1:T(8,128)} async-done(((f32[128,128]{0,1:T(8,128)}), f32[4096,128]{0,1:T(8,128)}) %all-gather.7.cloned.1.call-update) | async-done | bytes 2097168 | tf_op jit(solution)/shard_map/all_gather | solution.py:52
  187.5 14.0 %all-gather.1 = f32[1024,128]{0,1:T(8,128)S(1)} all-gather(f32[128,128]{0,1:T(8,128)S(1)} %bitcast_reduce_fusion.1), channel_id=3, replica_groups=mesh['leaf'=32,'sub'=8] {'sub'}, dimensions={0}, use_global_device_ids=true | all-gather | bytes 589824 | tf_op jit(solution)/shard_map/all_gather | solution.py:53
  243.8 4.7 collective-permute-done.20
  255.1 4.6 collective-permute-start.22
  265.1 5.9 %collective-permute-done.23 = f32[128,128]{0,1:T(8,128)S(1)} collective-permute-done((f32[128,128]{0,1:T(8,128)S(1)}, f32[128,128]{0,1:T(8,128)S(1)}, u32[]{:S(2)}, u32[]{:S(2)}) %collective-permute-start.23) | collective-permute-done | bytes 65568 | tf_op jit(solution)/shard_map/ppermute | solution.py:11
  271.1 4.2 collective-permute-done.24
  290.3 6.2 %collective-permute-done.27 = f32[128,128]{0,1:T(8,128)S(1)} collective-permute-done((f32[128,128]{0,1:T(8,128)S(1)}, f32[128,128]{0,1:T(8,128)S(1)}, u32[]{:S(2)}, u32[]{:S(2)}) %collective-permute-start.27) | collective-permute-done | bytes 65568 | tf_op jit(solution)/shard_map/ppermute | solution.py:11
  296.6 4.3 collective-permute-done.28
  310.1 73.5 %all-gather.9.cloned.1.call-done = f32[4096,128]{0,1:T(8,128)} async-done(((f32[128,128]{0,1:T(8,128)}), f32[4096,128]{0,1:T(8,128)}) %all-gather.9.cloned.1.call-update) | async-done | bytes 2097168 | tf_op jit(solution)/shard_map/all_gather | solution.py:52
  386.0 13.8 %all-gather.3 = f32[1024,128]{0,1:T(8,128)S(1)} all-gather(f32[128,128]{0,1:T(8,128)S(1)} %bitcast_reduce_fusion), channel_id=5, replica_groups=mesh['leaf'=32,'sub'=8] {'sub'}, dimensions={0}, use_global_device_ids=true | all-gather | bytes 589824 | tf_op jit(solution)/shard_map/all_gather | solution.py:53
  441.4 4.8 collective-permute-done.35
  452.7 4.3 collective-permute-start.37
  462.8 5.5 %collective-permute-done.38 = f32[128,128]{0,1:T(8,128)S(1)} collective-permute-done((f32[128,128]{0,1:T(8,128)S(1)}, f32[128,128]{0,1:T(8,128)S(1)}, u32[]{:S(2)}, u32[]{:S(2)}) %collective-permute-start.38) | collective-permute-done | bytes 65568 | tf_op jit(solution)/shard_map/ppermute | solution.py:11
  468.7 3.9 collective-permute-done.39
  487.9 4.7 collective-permute-done.42
  493.0 3.9 collective-permute-done.43
  499.0 3.7 collective-permute-done.44
  (196 shorter events, 224.0 us)
Async XLA Ops:
  6.5 178.7 %all-gather.7.cloned.1.call-start = ((), (), s32[]{:S(2)}) async-start(), calls=%async_computation | async-start | bytes 2162688 | tf_op jit(solution)/shard_map/all_gather | solution.py:52
  22.8 5.6 %collective-permute-start.2 = (f32[128,128]{0,1:T(8,128)S(1)}, f32[128,128]{0,1:T(8,128)S(1)}, u32[]{:S(2)}, u32[]{:S(2)}) collective-permute-start(f32[128,128]{0,1:T(8,128)S(1)} %add.154), channel_id=1, source_target_pairs={{0,16},{8,24},{16,0},{24,8},{32,48},{40,56},{48,32},{56,40},{64,80... | collective-permute-start | bytes 196616 | tf_op jit(solution)/shard_map/ppermute | solution.py:11
  35.3 5.3 %collective-permute-start.4 = (f32[128,128]{0,1:T(8,128)S(1)}, f32[128,128]{0,1:T(8,128)S(1)}, u32[]{:S(2)}, u32[]{:S(2)}) collective-permute-start(f32[128,128]{0,1:T(8,128)S(1)} %add.156), channel_id=1, source_target_pairs={{0,16},{8,24},{16,0},{24,8},{32,48},{40,56},{48,32},{56,40},{64,80... | collective-permute-start | bytes 196616 | tf_op jit(solution)/shard_map/ppermute | solution.py:11
  40.6 9.8 %collective-permute-start.5 = (f32[128,128]{0,1:T(8,128)S(1)}, f32[128,128]{0,1:T(8,128)S(1)}, u32[]{:S(2)}, u32[]{:S(2)}) collective-permute-start(f32[128,128]{0,1:T(8,128)S(1)} %add.157), channel_id=1, source_target_pairs={{0,32},{8,40},{16,48},{24,56},{32,0},{40,8},{48,16},{56,24},{64,96... | collective-permute-start | bytes 196616 | tf_op jit(solution)/shard_map/ppermute | solution.py:11
  56.9 6.6 %collective-permute-start.7 = (f32[128,128]{0,1:T(8,128)S(1)}, f32[128,128]{0,1:T(8,128)S(1)}, u32[]{:S(2)}, u32[]{:S(2)}) collective-permute-start(f32[128,128]{0,1:T(8,128)S(1)} %add.159), channel_id=1, source_target_pairs={{0,16},{8,24},{16,0},{24,8},{32,48},{40,56},{48,32},{56,40},{64,80... | collective-permute-start | bytes 196616 | tf_op jit(solution)/shard_map/ppermute | solution.py:11
  63.6 8.3 %collective-permute-start.8 = (f32[128,128]{0,1:T(8,128)S(1)}, f32[128,128]{0,1:T(8,128)S(1)}, u32[]{:S(2)}, u32[]{:S(2)}) collective-permute-start(f32[128,128]{0,1:T(8,128)S(1)} %add.160), channel_id=1, source_target_pairs={{0,32},{8,40},{16,48},{24,56},{32,0},{40,8},{48,16},{56,24},{64,96... | collective-permute-start | bytes 196616 | tf_op jit(solution)/shard_map/ppermute | solution.py:11
  83.3 5.3 %collective-permute-start.11 = (f32[128,128]{0,1:T(8,128)S(1)}, f32[128,128]{0,1:T(8,128)S(1)}, u32[]{:S(2)}, u32[]{:S(2)}) collective-permute-start(f32[128,128]{0,1:T(8,128)S(1)} %add.163), channel_id=1, source_target_pairs={{0,16},{8,24},{16,0},{24,8},{32,48},{40,56},{48,32},{56,40},{64,80... | collective-permute-start | bytes 196616 | tf_op jit(solution)/shard_map/ppermute | solution.py:11
  88.5 8.3 %collective-permute-start.12 = (f32[128,128]{0,1:T(8,128)S(1)}, f32[128,128]{0,1:T(8,128)S(1)}, u32[]{:S(2)}, u32[]{:S(2)}) collective-permute-start(f32[128,128]{0,1:T(8,128)S(1)} %add.164), channel_id=1, source_target_pairs={{0,32},{8,40},{16,48},{24,56},{32,0},{40,8},{48,16},{56,24},{64,96... | collective-permute-start | bytes 196616 | tf_op jit(solution)/shard_map/ppermute | solution.py:11
  101.2 5.9 %collective-permute-start.14 = (f32[128,128]{0,1:T(8,128)S(1)}, f32[128,128]{0,1:T(8,128)S(1)}, u32[]{:S(2)}, u32[]{:S(2)}) collective-permute-start(f32[128,128]{0,1:T(8,128)S(1)} %add.166), channel_id=1, source_target_pairs={{0,128},{8,136},{16,144},{24,152},{32,160},{40,168},{48,176},{56,1... | collective-permute-start | bytes 196616 | tf_op jit(solution)/shard_map/ppermute | solution.py:11
  109.6 274.1 %all-gather.9.cloned.1.call-start = ((), (), s32[]{:S(2)}) async-start(), calls=%async_computation.1 | async-start | bytes 2162688 | tf_op jit(solution)/shard_map/all_gather | solution.py:52
  234.7 5.5 %collective-permute-start.19 = (f32[128,128]{0,1:T(8,128)S(1)}, f32[128,128]{0,1:T(8,128)S(1)}, u32[]{:S(2)}, u32[]{:S(2)}) collective-permute-start(f32[128,128]{0,1:T(8,128)S(1)} %add.173), channel_id=1, source_target_pairs={{0,16},{8,24},{16,0},{24,8},{32,48},{40,56},{48,32},{56,40},{64,80... | collective-permute-start | bytes 196616 | tf_op jit(solution)/shard_map/ppermute | solution.py:11
  240.2 8.3 %collective-permute-start.20 = (f32[128,128]{0,1:T(8,128)S(1)}, f32[128,128]{0,1:T(8,128)S(1)}, u32[]{:S(2)}, u32[]{:S(2)}) collective-permute-start(f32[128,128]{0,1:T(8,128)S(1)} %add.174), channel_id=1, source_target_pairs={{0,32},{8,40},{16,48},{24,56},{32,0},{40,8},{48,16},{56,24},{64,96... | collective-permute-start | bytes 196616 | tf_op jit(solution)/shard_map/ppermute | solution.py:11
  255.1 7.5 %collective-permute-start.22 = (f32[128,128]{0,1:T(8,128)S(1)}, f32[128,128]{0,1:T(8,128)S(1)}, u32[]{:S(2)}, u32[]{:S(2)}) collective-permute-start(f32[128,128]{0,1:T(8,128)S(1)} %add.176), channel_id=1, source_target_pairs={{0,16},{8,24},{16,0},{24,8},{32,48},{40,56},{48,32},{56,40},{64,80... | collective-permute-start | bytes 196616 | tf_op jit(solution)/shard_map/ppermute | solution.py:11
  262.6 8.4 %collective-permute-start.23 = (f32[128,128]{0,1:T(8,128)S(1)}, f32[128,128]{0,1:T(8,128)S(1)}, u32[]{:S(2)}, u32[]{:S(2)}) collective-permute-start(f32[128,128]{0,1:T(8,128)S(1)} %add.177), channel_id=1, source_target_pairs={{0,32},{8,40},{16,48},{24,56},{32,0},{40,8},{48,16},{56,24},{64,96... | collective-permute-start | bytes 196616 | tf_op jit(solution)/shard_map/ppermute | solution.py:11
  282.3 6.0 %collective-permute-start.26 = (f32[128,128]{0,1:T(8,128)S(1)}, f32[128,128]{0,1:T(8,128)S(1)}, u32[]{:S(2)}, u32[]{:S(2)}) collective-permute-start(f32[128,128]{0,1:T(8,128)S(1)} %add.180), channel_id=1, source_target_pairs={{0,16},{8,24},{16,0},{24,8},{32,48},{40,56},{48,32},{56,40},{64,80... | collective-permute-start | bytes 196616 | tf_op jit(solution)/shard_map/ppermute | solution.py:11
  288.3 8.3 %collective-permute-start.27 = (f32[128,128]{0,1:T(8,128)S(1)}, f32[128,128]{0,1:T(8,128)S(1)}, u32[]{:S(2)}, u32[]{:S(2)}) collective-permute-start(f32[128,128]{0,1:T(8,128)S(1)} %add.181), channel_id=1, source_target_pairs={{0,32},{8,40},{16,48},{24,56},{32,0},{40,8},{48,16},{56,24},{64,96... | collective-permute-start | bytes 196616 | tf_op jit(solution)/shard_map/ppermute | solution.py:11
  300.9 5.9 %collective-permute-start.29 = (f32[128,128]{0,1:T(8,128)S(1)}, f32[128,128]{0,1:T(8,128)S(1)}, u32[]{:S(2)}, u32[]{:S(2)}) collective-permute-start(f32[128,128]{0,1:T(8,128)S(1)} %add.183), channel_id=1, source_target_pairs={{0,128},{8,136},{16,144},{24,152},{32,160},{40,168},{48,176},{56,1... | collective-permute-start | bytes 196616 | tf_op jit(solution)/shard_map/ppermute | solution.py:11
  432.2 5.8 %collective-permute-start.34 = (f32[128,128]{0,1:T(8,128)S(1)}, f32[128,128]{0,1:T(8,128)S(1)}, u32[]{:S(2)}, u32[]{:S(2)}) collective-permute-start(f32[128,128]{0,1:T(8,128)S(1)} %add.191), channel_id=1, source_target_pairs={{0,16},{8,24},{16,0},{24,8},{32,48},{40,56},{48,32},{56,40},{64,80... | collective-permute-start | bytes 196616 | tf_op jit(solution)/shard_map/ppermute | solution.py:11
  438.0 8.3 %collective-permute-start.35 = (f32[128,128]{0,1:T(8,128)S(1)}, f32[128,128]{0,1:T(8,128)S(1)}, u32[]{:S(2)}, u32[]{:S(2)}) collective-permute-start(f32[128,128]{0,1:T(8,128)S(1)} %add.192), channel_id=1, source_target_pairs={{0,32},{8,40},{16,48},{24,56},{32,0},{40,8},{48,16},{56,24},{64,96... | collective-permute-start | bytes 196616 | tf_op jit(solution)/shard_map/ppermute | solution.py:11
  452.7 7.2 %collective-permute-start.37 = (f32[128,128]{0,1:T(8,128)S(1)}, f32[128,128]{0,1:T(8,128)S(1)}, u32[]{:S(2)}, u32[]{:S(2)}) collective-permute-start(f32[128,128]{0,1:T(8,128)S(1)} %add.194), channel_id=1, source_target_pairs={{0,16},{8,24},{16,0},{24,8},{32,48},{40,56},{48,32},{56,40},{64,80... | collective-permute-start | bytes 196616 | tf_op jit(solution)/shard_map/ppermute | solution.py:11
  460.0 8.3 %collective-permute-start.38 = (f32[128,128]{0,1:T(8,128)S(1)}, f32[128,128]{0,1:T(8,128)S(1)}, u32[]{:S(2)}, u32[]{:S(2)}) collective-permute-start(f32[128,128]{0,1:T(8,128)S(1)} %add.195), channel_id=1, source_target_pairs={{0,32},{8,40},{16,48},{24,56},{32,0},{40,8},{48,16},{56,24},{64,96... | collective-permute-start | bytes 196616 | tf_op jit(solution)/shard_map/ppermute | solution.py:11
  479.0 5.3 %collective-permute-start.41 = (f32[128,128]{0,1:T(8,128)S(1)}, f32[128,128]{0,1:T(8,128)S(1)}, u32[]{:S(2)}, u32[]{:S(2)}) collective-permute-start(f32[128,128]{0,1:T(8,128)S(1)} %add.198), channel_id=1, source_target_pairs={{0,16},{8,24},{16,0},{24,8},{32,48},{40,56},{48,32},{56,40},{64,80... | collective-permute-start | bytes 196616 | tf_op jit(solution)/shard_map/ppermute | solution.py:11
  484.3 8.3 %collective-permute-start.42 = (f32[128,128]{0,1:T(8,128)S(1)}, f32[128,128]{0,1:T(8,128)S(1)}, u32[]{:S(2)}, u32[]{:S(2)}) collective-permute-start(f32[128,128]{0,1:T(8,128)S(1)} %add.199), channel_id=1, source_target_pairs={{0,32},{8,40},{16,48},{24,56},{32,0},{40,8},{48,16},{56,24},{64,96... | collective-permute-start | bytes 196616 | tf_op jit(solution)/shard_map/ppermute | solution.py:11
  496.9 5.9 %collective-permute-start.44 = (f32[128,128]{0,1:T(8,128)S(1)}, f32[128,128]{0,1:T(8,128)S(1)}, u32[]{:S(2)}, u32[]{:S(2)}) collective-permute-start(f32[128,128]{0,1:T(8,128)S(1)} %add.201), channel_id=1, source_target_pairs={{0,128},{8,136},{16,144},{24,152},{32,160},{40,168},{48,176},{56,1... | collective-permute-start | bytes 196616 | tf_op jit(solution)/shard_map/ppermute | solution.py:11
  (38 other events, 294.4 us)
Sparse Core Ops, SparseCore 0:
  109.7 75.4 all-gather.6
  310.3 73.3 all-gather.8
